TPU v7x, 256 devices: a whole 4x4x8 slice. The times are simulated.
256 devices in a mesh: tm: 64 (over x, y_hi, z), corpus: 4 (over y_lo, core).
Axes of the slice: x: 4, y: 4 (y_hi: 2, y_lo: 2; y = y_hi * 2 + y_lo), z: 8, core: 2. Of those that a mesh axis runs over, the one named last changes fastest.
Arguments:
- wave: float32 [4, 33554432], P('corpus', 'tm'), may hold values from -40 to 40, as said below
- dict_init: float32 [1025, 512], replicated, may hold values from 0.01 to 0.1
- act_init: float32 [4, 512, 32768], P('corpus', None, 'tm'), may hold values from 0.25 to 2.5
Outputs:
- dictionary: float32 [1025, 512], replicated
- activations: float32 [4, 512, 32768], P('corpus', None, 'tm')
Inputs may be any that keep to these rules, and one draw needn't show every extreme that they name: `wave`: waveform samples.
All inputs are finite; a program needn't handle non-finite values.
Results may differ from a plain program's by a relative error of at most 0.00048.
Values sent between devices are 32-bit elements; how exact they have to be, the bound alone decides.
A program may use at most 64 MiB of HBM per device.

v0:
```python
import jax
import jax.numpy as jnp
from jax import lax
from jax.sharding import PartitionSpec as P

WIN = 2048
HOP = 1024
BINS = 1025
ITERS = 3


HI = lax.Precision.HIGHEST


def shifted(value, axis, steps):
    count = lax.axis_size(axis)
    first, last = (max(0, -steps), min(count, count - steps))
    return lax.ppermute(value, axis, [(source, source + steps) for source in range(first, last)])


def make_table():
    index_n = jnp.arange(WIN, dtype=jnp.int32)[None, :]
    index_k = jnp.arange(BINS, dtype=jnp.int32)[:, None]
    phase = (index_k * index_n % WIN).astype(jnp.float32) * (2.0 * jnp.pi / WIN)
    return jnp.concatenate([jnp.cos(phase), jnp.sin(phase)], 0).astype(jnp.bfloat16)


def per_device(wave, dict_init, act_init):
    rows = wave[0].reshape(-1, HOP)
    follow = shifted(rows[0:1], "tm", -1)
    index_n = jnp.arange(WIN, dtype=jnp.float32)
    window = 0.5 - 0.5 * jnp.cos(2.0 * jnp.pi * index_n / WIN)
    ext = jnp.concatenate([rows, follow], 0)
    frames = (jnp.concatenate([ext[:-1], ext[1:]], 1) * window[None, :]).astype(jnp.bfloat16)
    spec = lax.dot_general(
        make_table(), frames, (((1,), (1,)), ((), ())), preferred_element_type=jnp.float32
    )
    mag = jnp.sqrt(spec[:BINS] ** 2 + spec[BINS:] ** 2 + 0.01)
    dictionary = dict_init
    activations = act_init[0]
    for step in range(ITERS):
        approx = jnp.dot(dictionary, activations, precision=HI)
        ratio = mag / approx
        colsum = jnp.sum(dictionary, 0)
        update = lax.dot_general(dictionary, ratio, (((0,), (0,)), ((), ())), precision=HI)
        activations = activations * update / colsum[:, None]
        approx = jnp.dot(dictionary, activations, precision=HI)
        ratio = mag / approx
        numer = lax.dot_general(ratio, activations, (((1,), (1,)), ((), ())), precision=HI)
        hsum = jnp.sum(activations, 1)
        numer, hsum = lax.psum((numer, hsum), ("tm", "corpus"))
        dictionary = dictionary * numer / hsum[None, :]
    return (dictionary, activations[None])


def solution(mesh):
    in_specs = (P("corpus", "tm"), P(), P("corpus", None, "tm"))
    out_specs = (P(), P("corpus", None, "tm"))
    return jax.shard_map(
        per_device, mesh=mesh, in_specs=in_specs, out_specs=out_specs, check_vma=False
    )
```

profile of v0, /device:TPU:1, one launch (start us, length us, event | category | flops | bytes accessed | tf_op | source)
XLA Modules:
  0.0 928.8 jit_solution(6000782653119349788)
XLA Ops:
  7.2 0.0 all-reduce.4.cloned.1.call-start
  7.2 0.7 slice.13
  7.9 1.4 collective-permute-start
  9.3 35.1 %sine_convert_fusion = (bf16[1025,2048]{1,0:T(8,128)(2,1)}, bf16[1025,2048]{1,0:T(8,128)(2,1)}) fusion(), kind=kLoop, calls=%fused_computation.6 | loop fusion | flops 33587200 | bytes 8396800 | tf_op jit(solution)/shard_map/convert.1
  44.4 0.1 multiply_subtract_fusion
  44.5 0.5 broadcast.41
  45.0 17.2 %reduce.3 = f32[524288]{0:T(1024)} reduce(f32[1,524288]{1,0:T(1,128)S(1)} %copy-done.8, f32[]{:T(128)} %broadcast.41), dimensions={0}, to_apply=%param.3.reduce_sub_computation.3 | reduce | bytes 4194308 | tf_op args[0]
  62.2 3.1 reshape_squeeze.3
  65.3 0.0 copy-done.9
  65.3 1.3 copy.5
  66.6 0.2 reduce_sum.54
  66.8 0.0 collective-permute-done
  66.8 9.5 %fusion.6 = f32[2050,512]{1,0:T(8,128)S(1)} fusion(bf16[1025,2048]{1,0:T(8,128)(2,1)} %get-tuple-element.14, bf16[1025,2048]{1,0:T(8,128)(2,1)} %get-tuple-element.15, f32[1,1024]{1,0:T(1,128)S(1)} %collective-permute-done, f32[512,1024]{1,0:T(8,128)} %reshape_squeeze.3, f32[2048]{0:T(1024)S(1)} %multiply_subtract_fusion), kind=kOutput, calls=%fused_computation.11 | convolution fusion | flops 4320149504 | bytes 14704640 | tf_op jit(solution)/shard_map/dot_general | solution.py:35
  76.3 0.9 fusion.16
  77.2 0.0 copy-start.5
  77.2 0.0 copy-start.4
  77.2 3.6 convolution_divide_fusion.4
  80.8 5.0 fusion.28
  85.8 0.0 copy-start.3
  85.8 0.0 copy-done.5
  85.8 3.6 fusion.13
  89.4 4.8 fusion.31
  94.2 0.0 all-reduce.4.cloned.1.call-update
  94.3 0.0 all-reduce.6.cloned.1.call-start
  94.3 84.6 %psum.43 = f32[512]{0:T(512)S(1)} all-reduce(f32[512]{0:T(512)S(1)} %get-tuple-element.8), channel_id=1, replica_groups=mesh['tm'=64,'corpus'=4] {'tm','corpus'}, use_global_device_ids=true, to_apply=%region_3.4 | all-reduce | flops 512 | bytes 4096 | tf_op jit(solution)/shard_map/psum | solution.py:51
  179.0 179.6 %all-reduce.4.cloned.1.call-done = f32[1025,512]{1,0:T(8,128)} async-done(((f32[1025,512]{1,0:T(8,128)}), f32[1025,512]{1,0:T(8,128)}) %all-reduce.4.cloned.1.call-update) | async-done | bytes 2099216 | tf_op jit(solution)/shard_map/psum | solution.py:51
  358.6 2.2 fusion.27
  360.8 0.0 copy-done.3
  360.8 0.0 copy-done.6
  360.8 3.6 convolution_divide_fusion.3
  364.5 5.8 fusion.29
  370.2 0.0 copy-start.2
  370.2 3.9 convolution_divide_fusion.2
  374.1 4.8 fusion.32
  378.9 0.0 all-reduce.6.cloned.1.call-update
  378.9 0.0 all-reduce.8.cloned.1.call-start
  379.0 78.6 %psum.45 = f32[512]{0:T(512)S(1)} all-reduce(f32[512]{0:T(512)S(1)} %get-tuple-element.10), channel_id=1, replica_groups=mesh['tm'=64,'corpus'=4] {'tm','corpus'}, use_global_device_ids=true, to_apply=%region_7.8 | all-reduce | flops 512 | bytes 4096 | tf_op jit(solution)/shard_map/psum | solution.py:51
  457.6 180.6 %all-reduce.6.cloned.1.call-done = f32[1025,512]{1,0:T(8,128)} async-done(((f32[1025,512]{1,0:T(8,128)}), f32[1025,512]{1,0:T(8,128)}) %all-reduce.6.cloned.1.call-update) | async-done | bytes 2099216 | tf_op jit(solution)/shard_map/psum | solution.py:51
  638.2 2.9 fusion.26
  641.1 3.6 convolution_divide_fusion.1
  644.8 5.7 fusion.30
  650.5 3.9 convolution_divide_fusion
  654.4 4.8 fusion.33
  659.2 0.0 all-reduce.8.cloned.1.call-update
  659.3 1.3 copy.6
  660.6 79.0 %psum.47 = f32[512]{0:T(512)S(1)} all-reduce(f32[512]{0:T(512)S(1)} %get-tuple-element.12), channel_id=1, replica_groups=mesh['tm'=64,'corpus'=4] {'tm','corpus'}, use_global_device_ids=true, to_apply=%region_11.12 | all-reduce | flops 512 | bytes 4096 | tf_op jit(solution)/shard_map/psum | solution.py:51
  739.6 178.8 %all-reduce.8.cloned.1.call-done = f32[1025,512]{1,0:T(8,128)} async-done(((f32[1025,512]{1,0:T(8,128)}), f32[1025,512]{1,0:T(8,128)}) %all-reduce.8.cloned.1.call-update) | async-done | bytes 2099216 | tf_op jit(solution)/shard_map/psum | solution.py:51
  918.4 3.4 multiply_divide_fusion
  (12 shorter events, 0.0 us)
Async XLA Ops:
  7.2 351.4 %all-reduce.4.cloned.1.call-start = ((), (), s32[]{:S(2)}) async-start(), calls=%async_computation | async-start | bytes 4227072 | tf_op jit(solution)/shard_map/psum | solution.py:51
  7.9 37.1 %copy-start.8 = (f32[1,524288]{1,0:T(1,128)S(1)}, f32[1,524288]{1,0:T(1,128)}, u32[]{:S(2)}) copy-start(f32[1,524288]{1,0:T(1,128)} %param.3) | copy-start | bytes 6291460
  7.9 58.9 %collective-permute-start = (f32[1,1024]{1,0:T(1,128)S(1)}, f32[1,1024]{1,0:T(1,128)S(1)}, u32[]{:S(2)}, u32[]{:S(2)}) collective-permute-start(f32[1,1024]{1,0:T(1,128)S(1)} %slice.13), channel_id=1, source_target_pairs={{4,0},{8,4},{12,8},{16,12},{20,16},{24,20},{28,24},{32,28},{36,32}... | collective-permute-start | bytes 12296 | tf_op jit(solution)/shard_map/ppermute | solution.py:18
  62.2 3.1 copy-start.9
  62.2 4.4 copy-start
  77.2 8.6 copy-start.5
  77.2 3.6 copy-start.4
  85.8 275.0 %copy-start.3 = (f32[512,512]{0,1:T(8,128)}, f32[512,512]{0,1:T(8,128)S(1)}, u32[]{:S(2)}) copy-start(f32[512,512]{0,1:T(8,128)S(1)} %get-tuple-element.9) | copy-start | bytes 3145732
  94.3 543.9 %all-reduce.6.cloned.1.call-start = ((), (), s32[]{:S(2)}) async-start(), calls=%async_computation.1 | async-start | bytes 4227072 | tf_op jit(solution)/shard_map/psum | solution.py:51
  358.6 2.2 copy-start.6
  360.8 9.5 %copy-start.1 = (f32[1025,512]{1,0:T(8,128)}, f32[1025,512]{1,0:T(8,128)S(1)}, u32[]{:S(2)}) copy-start(f32[1025,512]{1,0:T(8,128)S(1)} %get-tuple-element.7) | copy-start | bytes 6297604
  370.2 270.9 %copy-start.2 = (f32[512,512]{0,1:T(8,128)}, f32[512,512]{0,1:T(8,128)S(1)}, u32[]{:S(2)}) copy-start(f32[512,512]{0,1:T(8,128)S(1)} %get-tuple-element.11) | copy-start | bytes 3145732
  378.9 539.5 %all-reduce.8.cloned.1.call-start = ((), (), s32[]{:S(2)}) async-start(), calls=%async_computation.2 | async-start | bytes 4227072 | tf_op jit(solution)/shard_map/psum | solution.py:51
  638.2 2.9 copy-start.7
Sparse Core Ops, SparseCore 0:
  94.4 264.1 all-reduce.3
  379.1 259.0 all-reduce.5
  659.4 259.0 all-reduce.7
where the time goes:
time: 936 us; the launch traced here: 929 us
  waiting for transfers between devices  539 us (58%)
  blocking collectives  242 us (26%)
  matrix products  62.6 us (7%)
  other arithmetic  61.9 us (7%)
  between operations  14.4 us (2%)
    psum x3, waiting for transfers between devices, per_device(): numer, hsum = lax.psum((numer, hsum), ('tm', 'corpus'))  539 us
    psum x3, blocking collectives, per_device(): numer, hsum = lax.psum((numer, hsum), ('tm', 'corpus'))  242 us
    another operation x1, other arithmetic  35.1 us
    dot_general x6, matrix products, per_device(): approx = jnp.dot(dictionary, activations, precision=HI)  22.3 us
  transfers between devices with their start and end apart: 4, of which 3 were waited for; matrix products, arithmetic and copies ran while one was open for 6% of the time, Pallas kernels for 0%

commit v1 on v0

v1 whole, which is shorter than its diff:
```python
import functools

import jax
import jax.numpy as jnp
import numpy as np
from jax import lax
from jax.experimental import pallas as pl
from jax.experimental.pallas import tpu as pltpu
from jax.sharding import PartitionSpec as P

WIN = 2048
HOP = 1024
BINS = 1025
K = 512
ITERS = 3
MESH = pl.DeviceIdType.MESH
F32 = jnp.float32
BF16 = jnp.bfloat16


def shifted(value, axis, steps):
    count = lax.axis_size(axis)
    first, last = (max(0, -steps), min(count, count - steps))
    return lax.ppermute(value, axis, [(source, source + steps) for source in range(first, last)])


def make_table():
    index_n = np.arange(WIN, dtype=np.int64)[None, :]
    index_k = np.arange(BINS, dtype=np.int64)[:, None]
    phase = (index_k * index_n % WIN).astype(np.float64) * (2.0 * np.pi / WIN)
    table = np.concatenate([np.cos(phase), np.sin(phase)], 0).astype(np.float32)
    return table.astype(jnp.bfloat16)


def device(x, y, z, k):
    return (x * 16 + (y // 2) * 8 + z, (y % 2) * 2 + k)


CORE, CORE_E = 0, 2
P1, P2, P3 = 3, 11, 19
E1, E2, E3 = 35, 39, 43
G3, G2, G1, GC = 51, 67, 75, 83
SEMS = 91


def nmf_kernel(
    mag, d0, a0, d_out, a_out,
    dland, dbf, debf, drow, abf, atbf, upd, csum,
    cs, cr, es, er, own,
    r1, r2, r3, s2, s3, re1, re2, re3, esum, ssem, rsem,
):
    tm, corpus = lax.axis_index("tm"), lax.axis_index("corpus")
    x, z, k = tm // 16, tm % 8, corpus % 2
    y = ((tm // 8) % 2) * 2 + corpus // 2
    core = device(x, y, z, 1 - k)

    def at_x(i):
        return device(i, y, z, k)

    def at_y(i):
        return device(x, i, z, k)

    def at_z(i):
        return device(x, y, i, k)

    axes = (((x, at_x), (y, at_y)), ((y, at_y), (x, at_x)))

    barrier = pltpu.get_barrier_semaphore()
    pl.semaphore_signal(barrier, inc=1, device_id=core, device_id_type=MESH)
    for d in range(1, 4):
        pl.semaphore_signal(barrier, inc=1, device_id=at_x((x + d) % 4), device_id_type=MESH)
        pl.semaphore_signal(barrier, inc=1, device_id=at_y((y + d) % 4), device_id_type=MESH)
    for d in range(1, 8):
        pl.semaphore_signal(barrier, inc=1, device_id=at_z((z + d) % 8), device_id_type=MESH)
    pl.semaphore_wait(barrier, 14)

    def copy(src, dst, send, recv, to):
        return pltpu.make_async_remote_copy(
            src_ref=src, dst_ref=dst, send_sem=ssem.at[send], recv_sem=rsem.at[recv],
            device_id=to, device_id_type=MESH,
        )

    def rows(start, count):
        return pl.ds(pl.multiple_of(start, count), count)

    def dot(a, b):
        return jnp.dot(a, b, preferred_element_type=F32)

    def dot_t(a, b):
        return lax.dot_general(a, b, (((0,), (0,)), ((), ())), preferred_element_type=F32)

    ones = jnp.ones((256, 128), BF16)
    row_id = lax.broadcasted_iota(jnp.int32, (16, K), 0)

    def row_of(tile):
        return jnp.concatenate([tile[i : i + 1, :] for i in range(4)], 1)

    def ratio_e():
        approx = dot(debf[...], abf[...])
        ratio = mag[1024:1025, :] / approx[0:1, :]
        return jnp.where(row_id == 0, ratio, jnp.where(row_id == 8, 1.0, 0.0)).astype(BF16)

    def set_row(row):
        drow[...] = row
        debf[...] = jnp.where(row_id == 0, row, 0.0).astype(BF16)

    def ratio_at(at):
        approx = dot(dbf[rows(at, 256), :], abf[...])
        return (mag[rows(at, 256), :] / approx).astype(BF16)

    def first_half(at):
        ratio = ratio_at(at)
        part = dbf[rows(at, 256), :]
        upd[...] += dot_t(part, ratio)
        csum[...] += dot_t(part, ones)

    def start_first_half():
        ratio = ratio_e()
        upd[...] = dot_t(debf[...], ratio)
        csum[...] = dot_t(debf[...], ones[0:16])

    def set_act():
        value = a_out[...]
        abf[...] = value.astype(BF16)
        atbf[...] = value.T.astype(BF16)

    def finish_first_half():
        scale = 1.0 / csum[...]
        for i in range(4):
            cols = slice(i * 128, i * 128 + 128)
            a_out[:, cols] = a_out[:, cols] * upd[:, cols] * scale
        set_act()

    a_out[...] = a0[...]
    abf[...] = a0[...].astype(BF16)
    dland[...] = d0[0:1024, :]
    dbf[...] = d0[0:1024, :].astype(BF16)
    set_row(d0[1024:1025, :])
    start_first_half()

    @pl.loop(0, 4)
    def _(c):
        first_half(c * 256)

    finish_first_half()

    tile_row = (z // 4) * 8
    tile_col = pl.ds(pl.multiple_of((z % 4) * 128, 128), 128)
    near = (2, 1, 3)
    near_z = (4, 3, 5, 2, 6, 1, 7)

    @pl.loop(0, ITERS)
    def _(t):
        sends = []

        def send(*args):
            c = copy(*args)
            c.start()
            sends.append(c)

        def arrived(dst, recv):
            copy(dst, dst, 0, recv, core).wait_recv()

        ratio = ratio_e()
        line = dot(ratio, atbf[...])
        es[...] = jnp.concatenate(
            [line[r : r + 1, i * 128 : i * 128 + 128] for r in (0, 8) for i in range(4)], 0
        )
        send(es, er, CORE_E, CORE_E, core)
        for p in range(2):
            part = slice(p * 256, p * 256 + 256)
            cs[part, :] = dot(ratio_at((1 - k) * 512 + p * 256), atbf[...])
            send(cs.at[part, :], cr.at[part, :], CORE + p, CORE + p, core)

        def exchange_e(base, dst, me, at, count, order):
            for d in order:
                to = (me + d) % count
                send(dst.at[me], dst.at[me], base + d, base + me, at(to))

        for p in range(2):
            me, at = axes[p][0]
            part = slice(p * 256, p * 256 + 256)
            value = dot(ratio_at(k * 512 + p * 256), atbf[...])
            arrived(cr.at[part, :], CORE + p)
            own[part, :] = value + cr[part, :]
            for d in near:
                to = (me + d) % 4
                send(
                    own.at[rows(p * 256 + to * 64, 64), :], r1.at[p, me],
                    P1 + p * 4 + d, P1 + p * 4 + me, at(to),
                )
            if p == 0:
                arrived(er, CORE_E)
                re1[x] = es[...] + er[...]
                exchange_e(E1, re1, x, at_x, 4, near)
            r1[p, me] = own[rows(p * 256 + me * 64, 64), :]

        for p in range(2):
            before = axes[p][0][0]
            me, at = axes[p][1]
            for d in (1, 3, 2):
                i = (before + d) % 4
                arrived(r1.at[p, i], P1 + p * 4 + i)
            s2[p] = (r1[p, 0] + r1[p, 1]) + (r1[p, 2] + r1[p, 3])
            for d in near:
                to = (me + d) % 4
                send(s2.at[p, rows(to * 16, 16), :], r2.at[p, me], P2 + p * 4 + d, P2 + p * 4 + me, at(to))
            if p == 0:
                for d in (1, 3, 2):
                    i = (x + d) % 4
                    arrived(re1.at[i], E1 + i)
                re2[y] = (re1[0] + re1[1]) + (re1[2] + re1[3])
                exchange_e(E2, re2, y, at_y, 4, near)
            r2[p, me] = s2[p, rows(me * 16, 16), :]

        for p in range(2):
            before = axes[p][1][0]
            for d in (1, 3, 2):
                i = (before + d) % 4
                arrived(r2.at[p, i], P2 + p * 4 + i)
            total = (r2[p, 0] + r2[p, 1]) + (r2[p, 2] + r2[p, 3])
            for i in range(8):
                s3[p, i] = total[(i // 4) * 8 : (i // 4) * 8 + 8, (i % 4) * 128 : (i % 4) * 128 + 128]
            for d in near_z:
                to = (z + d) % 8
                send(s3.at[p, to], r3.at[p, z], P3 + p * 8 + d, P3 + p * 8 + z, at_z(to))
            if p == 0:
                for d in (1, 3, 2):
                    i = (y + d) % 4
                    arrived(re2.at[i], E2 + i)
                re3[z] = (re2[0] + re2[1]) + (re2[2] + re2[3])
                exchange_e(E3, re3, z, at_z, 8, near_z)
            r3[p, z] = s3[p, z]

        base = [k * 512 + p * 256 + axes[p][0][0] * 64 for p in range(2)]
        small = [base[p] + axes[p][1][0] * 16 for p in range(2)]
        for p in range(2):
            for d in (1, 7, 2, 6, 3, 5, 4):
                i = (z + d) % 8
                arrived(r3.at[p, i], P3 + p * 8 + i)
            if p == 0:
                for d in (1, 7, 2, 6, 3, 5, 4):
                    i = (z + d) % 8
                    arrived(re3.at[i], E3 + i)
                esum[...] = ((re3[0] + re3[1]) + (re3[2] + re3[3])) + ((re3[4] + re3[5]) + (re3[6] + re3[7]))
            total = ((r3[p, 0] + r3[p, 1]) + (r3[p, 2] + r3[p, 3])) + ((r3[p, 4] + r3[p, 5]) + (r3[p, 6] + r3[p, 7]))
            tile = (rows(small[p] + tile_row, 8), tile_col)
            dland[tile] = dland[tile] * total / esum[pl.ds(4 + z % 4, 1), :]
            for d in near_z:
                to = (z + d) % 8
                send(dland.at[tile], dland.at[tile], G3 + p * 8 + d, G3 + p * 8 + z, at_z(to))

        esum_v = esum[...]
        set_row(drow[...] * row_of(esum_v[0:4, :]) / row_of(esum_v[4:8, :]))

        for p in range(2):
            me, at = axes[p][1]
            for d in (1, 7, 2, 6, 3, 5, 4):
                i = (z + d) % 8
                tile = (
                    rows(small[p] + (i // 4) * 8, 8),
                    pl.ds(pl.multiple_of((i % 4) * 128, 128), 128),
                )
                arrived(dland.at[tile], G3 + p * 8 + i)
            piece = dland.at[rows(small[p], 16), :]
            for d in near:
                to = (me + d) % 4
                send(piece, piece, G2 + p * 4 + d, G2 + p * 4 + me, at(to))

        for p in range(2):
            me, at = axes[p][0]
            second = axes[p][1][0]
            for d in (1, 3, 2):
                i = (second + d) % 4
                arrived(dland.at[rows(base[p] + i * 16, 16), :], G2 + p * 4 + i)
            piece = dland.at[rows(base[p], 64), :]
            for d in near:
                to = (me + d) % 4
                send(piece, piece, G1 + p * 4 + d, G1 + p * 4 + me, at(to))
            send(piece, piece, GC + p * 4, GC + p * 4 + me, core)

        for d in (1, 3, 2):
            for p in range(2):
                i = (axes[p][0][0] + d) % 4
                piece = dland.at[rows(k * 512 + p * 256 + i * 64, 64), :]
                arrived(piece, G1 + p * 4 + i)
                send(piece, piece, GC + p * 4 + d, GC + p * 4 + i, core)

        def consume(at):
            @pl.when(t < ITERS - 1)
            def _():
                dbf[rows(at, 256), :] = dland[rows(at, 256), :].astype(BF16)
                first_half(at)

        @pl.when(t < ITERS - 1)
        def _():
            start_first_half()

        for p in range(2):
            consume(k * 512 + p * 256)
        for p in range(2):
            for i in range(4):
                arrived(dland.at[rows((1 - k) * 512 + p * 256 + i * 64, 64), :], GC + p * 4 + i)
            consume((1 - k) * 512 + p * 256)

        @pl.when(t < ITERS - 1)
        def _():
            finish_first_half()

        for c in sends:
            c.wait_send()

    d_out[0:1024, :] = dland[...]
    d_out[1024:1025, :] = drow[...]


def nmf(mag, dictionary, activations):
    vmem = pl.BlockSpec(memory_space=pltpu.VMEM)
    return pl.pallas_call(
        nmf_kernel,
        out_shape=[
            jax.ShapeDtypeStruct((BINS, K), F32),
            jax.ShapeDtypeStruct((K, 512), F32),
        ],
        in_specs=[vmem] * 3,
        out_specs=[vmem] * 2,
        scratch_shapes=[
            pltpu.VMEM((1024, K), F32),
            pltpu.VMEM((1024, K), BF16),
            pltpu.VMEM((16, K), BF16),
            pltpu.VMEM((1, K), F32),
            pltpu.VMEM((K, 512), BF16),
            pltpu.VMEM((512, K), BF16),
            pltpu.VMEM((K, 512), F32),
            pltpu.VMEM((K, 128), F32),
            pltpu.VMEM((512, K), F32),
            pltpu.VMEM((512, K), F32),
            pltpu.VMEM((8, 128), F32),
            pltpu.VMEM((8, 128), F32),
            pltpu.VMEM((512, K), F32),
            pltpu.VMEM((2, 4, 64, K), F32),
            pltpu.VMEM((2, 4, 16, K), F32),
            pltpu.VMEM((2, 8, 8, 128), F32),
            pltpu.VMEM((2, 64, K), F32),
            pltpu.VMEM((2, 8, 8, 128), F32),
            pltpu.VMEM((4, 8, 128), F32),
            pltpu.VMEM((4, 8, 128), F32),
            pltpu.VMEM((8, 8, 128), F32),
            pltpu.VMEM((8, 128), F32),
            pltpu.SemaphoreType.DMA((SEMS,)),
            pltpu.SemaphoreType.DMA((SEMS,)),
        ],
        compiler_params=pltpu.CompilerParams(
            collective_id=0, has_side_effects=True, vmem_limit_bytes=48 * 2**20
        ),
        name="nmf",
    )(mag, dictionary, activations)


def per_device(wave, dict_init, act_init):
    rows = wave[0].reshape(-1, HOP)
    follow = shifted(rows[0:1], "tm", -1)
    index_n = np.arange(WIN, dtype=np.float64)
    window = jnp.asarray((0.5 - 0.5 * np.cos(2.0 * np.pi * index_n / WIN)).astype(np.float32))
    ext = jnp.concatenate([rows, follow], 0)
    frames = (jnp.concatenate([ext[:-1], ext[1:]], 1) * window[None, :]).astype(BF16)
    spec = lax.dot_general(
        jnp.asarray(make_table()), frames, (((1,), (1,)), ((), ())), preferred_element_type=F32
    )
    mag = jnp.sqrt(spec[:BINS] ** 2 + spec[BINS:] ** 2 + 0.01)
    dictionary, activations = nmf(mag, dict_init, act_init[0])
    return (dictionary, activations[None])


def solution(mesh):
    in_specs = (P("corpus", "tm"), P(), P("corpus", None, "tm"))
    out_specs = (P(), P("corpus", None, "tm"))
    return jax.shard_map(
        per_device, mesh=mesh, in_specs=in_specs, out_specs=out_specs, check_vma=False
    )
```

time: 936 us -> 174 us (0.19)
  waiting for transfers between devices: 539 us -> 0.01 us
  blocking collectives: 242 us -> 0 us
  Pallas kernels: 0 us -> 136 us
  matrix products: 62.6 us -> 9.43 us
  other arithmetic: 61.9 us -> 21.3 us
  between operations: 14.4 us -> 0.68 us
    psum x3 -> x0, waiting for transfers between devices: 539 us -> none  [per_device(): numer, hsum = lax.psum((numer, hsum), ('tm', 'corpus'))]
    psum x3 -> x0, blocking collectives: 242 us -> none  [per_device(): numer, hsum = lax.psum((numer, hsum), ('tm', 'corpus'))]
    pallas_call x0 -> x1, Pallas kernels: none -> 136 us  [nmf(): pl.pallas_call(nmf_kernel, out_shape=[jax.ShapeDtypeStruct((BINS, K), F32...]
    dot_general x13 -> x1, matrix products: 62.6 us -> 9.43 us  [per_device(): lax.dot_general(jnp.asarray(make_table()), frames, (((1,), (1,)), ((), ()...]
    another operation x1 -> x0, other arithmetic: 35.1 us -> none
  transfers between devices with their start and end apart: 4 -> 1, of which waited for: 3 -> 0; matrix products, arithmetic and copies ran while one was open for 6% -> 12% of each run, Pallas kernels for 0% -> 0%
where the time goes in v1:
time: 174 us
  Pallas kernels  136 us (78%)
  other arithmetic  21.3 us (12%)
  matrix products  9.43 us (5%)
  local copies, waits for them, and re-layouts  5 us (3%)
    pallas_call x1, Pallas kernels, nmf(): pl.pallas_call(nmf_kernel, out_shape=[jax.ShapeDtypeStruct((BINS, K), F32...  136 us
    unnamed x1, other arithmetic  19 us
    dot_general x1, matrix products, per_device(): lax.dot_general(jnp.asarray(make_table()), frames, (((1,), (1,)), ((), ()...  9.43 us
  transfers between devices with their start and end apart: 1, of which 0 were waited for; matrix products, arithmetic and copies ran while one was open for 12% of the time, Pallas kernels for 0%

profile of v1, /device:TPU:1, one launch (start us, length us, event | category | flops | bytes accessed | tf_op | source)
XLA Modules:
  0.0 173.8 jit_solution(6855882905663321400)
XLA Ops:
  0.6 0.7 slice.13
  1.3 1.3 collective-permute-start
  2.6 0.5 broadcast.4
  3.1 19.0 %reduce.3 = f32[524288]{0:T(1024)S(1)} reduce(f32[1,524288]{1,0:T(1,128)} %param.5, f32[]{:T(128)} %broadcast.4), dimensions={0}, to_apply=%param.5.reduce_sub_computation.3 | reduce | bytes 4194308 | tf_op args[0]
  22.2 0.0 copy-start.1
  22.2 1.5 reshape_squeeze.3
  23.7 0.0 collective-permute-done
  23.7 0.0 copy-done.1
  23.7 9.4 %fusion.6 = f32[2050,512]{1,0:T(8,128)S(1)} fusion(bf16[2050,2048]{1,0:T(8,128)(2,1)} %constant.7.clone, f32[1,1024]{1,0:T(1,128)S(1)} %collective-permute-done, f32[512,1024]{1,0:T(8,128)} %reshape_squeeze.3, f32[2048]{0:T(1024)S(1)} %copy-done.1), kind=kOutput, calls=%fused_computation.9 | convolution fusion | flops 4303355904 | bytes 14704640 | tf_op jit(solution)/shard_map/dot_general | solution.py:367
  33.1 0.0 copy-start
  33.1 2.2 %fusion.5.mag = f32[1025,512]{1,0:T(8,128)} fusion(f32[2050,512]{1,0:T(8,128)S(1)} %fusion.6), kind=kLoop, calls=%fused_computation.7 | loop fusion | flops 2099200 | bytes 6297600 | tf_op jit(solution)/shard_map/sqrt | solution.py:370
  35.3 0.0 copy-done
  35.3 136.1 %nmf.1 = (f32[1025,512]{1,0:T(8,128)S(1)}, f32[512,512]{1,0:T(8,128)S(1)}) custom-call(f32[1025,512]{1,0:T(8,128)} %fusion.5.mag, f32[1025,512]{1,0:T(8,128)} %d0.1, f32[512,512]{1,0:T(8,128)S(1)} %bitcast.3), custom_call_target="tpu_custom_call" | custom-call | tf_op jit(solution)/shard_map/nmf/pallas_call | solution.py:319
  171.5 1.3 copy.9
  172.8 1.0 copy.10
Async XLA Ops:
  1.3 22.4 %collective-permute-start = (f32[1,1024]{1,0:T(1,128)S(1)}, f32[1,1024]{1,0:T(1,128)S(1)}, u32[]{:S(2)}, u32[]{:S(2)}) collective-permute-start(f32[1,1024]{1,0:T(1,128)S(1)} %slice.13), channel_id=1, source_target_pairs={{4,0},{8,4},{12,8},{16,12},{20,16},{24,20},{28,24},{32,28},{36,32}... | collective-permute-start | bytes 12296 | tf_op jit(solution)/shard_map/ppermute | solution.py:24
  22.2 1.5 copy-start.1
  33.1 2.2 %copy-start = (f32[1,512,512]{2,1,0:T(8,128)S(1)}, f32[1,512,512]{2,1,0:T(8,128)}, u32[]{:S(2)}) copy-start(f32[1,512,512]{2,1,0:T(8,128)} %param.7) | copy-start | bytes 3145732

commit v2 on v1

v2 whole, which is shorter than its diff:
```python
import functools

import jax
import jax.numpy as jnp
import numpy as np
from jax import lax
from jax.experimental import pallas as pl
from jax.experimental.pallas import tpu as pltpu
from jax.sharding import PartitionSpec as P

WIN = 2048
HOP = 1024
BINS = 1025
K = 512
ITERS = 3
MESH = pl.DeviceIdType.MESH
F32 = jnp.float32
BF16 = jnp.bfloat16


def make_table():
    index_n = np.arange(WIN, dtype=np.int64)[None, :]
    index_k = np.arange(BINS, dtype=np.int64)[:, None]
    phase = (index_k * index_n % WIN).astype(np.float64) * (2.0 * np.pi / WIN)
    last = np.zeros((16, WIN))
    last[0], last[8] = np.cos(phase[BINS - 1]), np.sin(phase[BINS - 1])
    table = np.concatenate([np.cos(phase[: BINS - 1]), np.sin(phase[: BINS - 1]), last], 0)
    return table.astype(np.float32).astype(jnp.bfloat16)


def make_window():
    index_n = np.arange(WIN, dtype=np.float64)
    return (0.5 - 0.5 * np.cos(2.0 * np.pi * index_n / WIN)).astype(np.float32).reshape(16, 128)


def device(x, y, z, k):
    return (x * 16 + (y // 2) * 8 + z, (y % 2) * 2 + k)


CORE, CORE_E = 0, 4
P1, P2, P3 = 5, 13, 15
E1, E2, E3 = 17, 18, 19
G3, G2, G1, GC = 20, 22, 30, 38
SEMS = 46


def atom_scale(index):
    value = index * 0.6180339887
    return 1.0 + (value - jnp.floor(value))


def nmf_kernel(
    wave, table, window, d0, a0, d_out, a_out,
    samples, frames, halo, tail, tab, spec, mag,
    dland, dbf, debf, drow, abf, atbf, upd, csum,
    cs, cr, es, er, own,
    r1, r2, r3, s2, s3, re1, re2, re3, esum, ssem, rsem, lsem, hsem,
):
    tm, corpus = lax.axis_index("tm"), lax.axis_index("corpus")
    x, z, k = tm // 16, tm % 8, corpus % 2
    y = ((tm // 8) % 2) * 2 + corpus // 2
    core = device(x, y, z, 1 - k)

    def at_x(i):
        return device(i, y, z, k)

    def at_y(i):
        return device(x, i, z, k)

    def at_z(i):
        return device(x, y, i, k)

    axes = (((x, at_x), (y, at_y)), ((y, at_y), (x, at_x)))

    loads = [
        pltpu.make_async_copy(wave, samples.at[0:4096, :], lsem.at[0]),
        pltpu.make_async_copy(d0.at[0:1024, :], dland, lsem.at[1]),
        pltpu.make_async_copy(a0, a_out, lsem.at[2]),
    ]
    for c in range(4):
        for h in range(2):
            part = slice(h * 1024 + c * 256, h * 1024 + c * 256 + 256)
            loads.append(pltpu.make_async_copy(table.at[part, :], tab.at[part, :], lsem.at[3 + 2 * c + h]))
    loads.append(pltpu.make_async_copy(table.at[2048:2064, :], tab.at[2048:2064, :], lsem.at[11]))
    loads.append(pltpu.make_async_copy(d0.at[1024:1025, :], drow, lsem.at[12]))
    for i in (0, 3, 4, 11, 5, 6, 7, 8, 9, 10, 2, 1, 12):
        loads[i].start()

    barrier = pltpu.get_barrier_semaphore()
    before, after = ((tm + 63) % 64, corpus), ((tm + 1) % 64, corpus)
    for neighbour in (before, after):
        pl.semaphore_signal(barrier, inc=1, device_id=neighbour, device_id_type=MESH)
    pl.semaphore_signal(barrier, inc=1, device_id=core, device_id_type=MESH)
    for d in range(1, 4):
        pl.semaphore_signal(barrier, inc=1, device_id=at_x((x + d) % 4), device_id_type=MESH)
        pl.semaphore_signal(barrier, inc=1, device_id=at_y((y + d) % 4), device_id_type=MESH)
    for d in range(1, 8):
        pl.semaphore_signal(barrier, inc=1, device_id=at_z((z + d) % 8), device_id_type=MESH)

    def copy(src, dst, send, recv, to):
        return pltpu.make_async_remote_copy(
            src_ref=src, dst_ref=dst, send_sem=ssem.at[send], recv_sem=rsem.at[recv],
            device_id=to, device_id_type=MESH,
        )

    def rows(start, count, step=None):
        return pl.ds(pl.multiple_of(start, step or count), count)

    def dot(a, b):
        return jnp.dot(a, b, preferred_element_type=F32)

    def dot_t(a, b):
        return lax.dot_general(a, b, (((0,), (0,)), ((), ())), preferred_element_type=F32)

    def dot_nt(a, b):
        return lax.dot_general(a, b, (((1,), (1,)), ((), ())), preferred_element_type=F32)

    def split(value):
        high = value.astype(BF16)
        return high, (value - high.astype(F32)).astype(BF16)

    row_id = lax.broadcasted_iota(jnp.int32, (16, K), 0)

    def row_of(tile):
        return jnp.concatenate([tile[i : i + 1, :] for i in range(4)], 1)

    def ratio_e():
        approx = dot(debf[0:16, :], abf[...])
        return mag[1024:1025, :] / approx[0:1, :]

    def set_row(row):
        drow[...] = row
        high, low = split(jnp.where(row_id == 0, row, 0.0))
        debf[0:16, :] = high
        debf[16:32, :] = low

    def products(high, low, ratio):
        rh, rl = split(ratio)
        left = jnp.concatenate([high, high, low], 0)
        update = dot_t(left, jnp.concatenate([rh, rl, rh], 0))
        count = high.shape[0]
        return update, dot_t(left[count:], jnp.ones((2 * count, 128), BF16))

    def first_half(high, low, target):
        ratio = target / dot(high, abf[...])
        update, total = products(high, low, ratio)
        upd[...] += update
        csum[...] += total

    def start_first_half():
        ratio = jnp.where(row_id == 0, ratio_e(), 0.0)
        update, total = products(debf[0:16, :], debf[16:32, :], ratio)
        upd[...] = update
        csum[...] = total

    def set_act():
        value = a_out[...]
        abf[...] = value.astype(BF16)
        atbf[...] = value.T.astype(BF16)

    def finish_first_half():
        scale = 1.0 / csum[...]
        for i in range(4):
            cols = slice(i * 128, i * 128 + 128)
            a_out[:, cols] = a_out[:, cols] * upd[:, cols] * scale
        set_act()

    loads[0].wait()
    for c in range(8):
        cols = slice(c * 128, c * 128 + 128)
        frames[:, cols] = (samples[pl.ds(c, 512, stride=8), :] * window[c : c + 1, :]).astype(BF16)
    samples[4096:4104, :] = jnp.zeros((8, 128), F32)
    for c in range(8):
        cols = slice(1024 + c * 128, 1024 + c * 128 + 128)
        frames[:, cols] = (samples[pl.ds(8 + c, 512, stride=8), :] * window[8 + c : 9 + c, :]).astype(BF16)

    for c in range(4):
        if c == 1:
            pl.semaphore_wait(barrier, 16)
            greet = pltpu.make_async_remote_copy(
                src_ref=samples.at[0:8, :], dst_ref=halo, send_sem=hsem.at[0], recv_sem=hsem.at[1],
                device_id=before, device_id_type=MESH,
            )
            greet.start()
        for h in range(2):
            part = slice(h * 1024 + c * 256, h * 1024 + c * 256 + 256)
            loads[3 + 2 * c + h].wait()
            spec[part, :] = dot_nt(tab[part, :], frames[...])
    loads[11].wait()
    spec[2048:2064, :] = dot_nt(tab[2048:2064, :], frames[...])

    loads[1].wait()
    loads[2].wait()
    loads[12].wait()
    atom_row = lax.broadcasted_iota(jnp.int32, (8, K), 1).astype(F32)[0:1]
    atom_col = lax.broadcasted_iota(jnp.int32, (K, 128), 0).astype(F32)
    inverse = 1.0 / atom_scale(atom_row)
    scale = atom_scale(atom_col)
    for i in range(4):
        cols = slice(i * 128, i * 128 + 128)
        value = a_out[:, cols] * scale
        a_out[:, cols] = value
        abf[:, cols] = value.astype(BF16)

    set_row(drow[...] * inverse)

    greet.wait()
    keep = jnp.where(tm == 63, 0.0, 1.0)
    tail[...] = jnp.zeros((128, 1024), BF16)
    last = halo[...] * window[8:16, :] * keep
    last = jnp.concatenate([last[c : c + 1, :] for c in range(8)], 1)
    row_16 = lax.broadcasted_iota(jnp.int32, (16, 1024), 0)
    tail[112:128, :] = jnp.where(row_16 == 15, last, 0.0).astype(BF16)
    spec[:, 384:512] += dot_nt(tab[:, 1024:2048], tail[...])

    real, imag = spec[2048:2049, :], spec[2056:2057, :]
    mag[1024:1025, :] = jnp.sqrt(real * real + imag * imag + 0.01)
    start_first_half()

    @pl.loop(0, 4)
    def _(c):
        real, imag = spec[rows(c * 256, 256), :], spec[rows(1024 + c * 256, 256), :]
        target = jnp.sqrt(real * real + imag * imag + 0.01)
        mag[rows(c * 256, 256), :] = target
        value = dland[rows(c * 256, 256), :] * inverse
        dland[rows(c * 256, 256), :] = value
        high, low = split(value)
        dbf[rows(c * 256, 256), :] = high
        first_half(high, low, target)

    finish_first_half()

    tile_row = (z // 4) * 8
    tile_col = pl.ds(pl.multiple_of((z % 4) * 128, 128), 128)
    near = (2, 1, 3)
    near_z = (4, 3, 5, 2, 6, 1, 7)

    @pl.loop(0, ITERS)
    def _(t):
        def send(*args):
            copy(*args).start()

        def arrived(dst, recv):
            copy(dst, dst, 0, recv, core).wait_recv()

        def left(src, sent):
            copy(src, src, sent, 0, core).wait_send()

        def group(half, jd):
            return [
                half * 512 + p * 256 + i * 64 + ((axes[p][1][0] + jd) % 4) * 16
                for p in range(2)
                for i in range(4)
            ]

        def gather(ref, starts):
            return jnp.concatenate([ref[rows(start, 16), :] for start in starts], 0)

        def numerator(half, jd):
            starts = group(half, jd)
            ratio = gather(mag, starts) / dot(gather(dbf, starts), abf[...])
            return dot(ratio.astype(BF16), atbf[...])

        def exchange_e(sem, dst, me, at, count, order):
            for d in order:
                send(dst.at[me], dst.at[me], sem, sem, at((me + d) % count))

        ratio = jnp.where(row_id == 0, ratio_e(), jnp.where(row_id == 8, 1.0, 0.0)).astype(BF16)
        line = dot(ratio, atbf[...])
        es[...] = jnp.concatenate(
            [line[r : r + 1, i * 128 : i * 128 + 128] for r in (0, 8) for i in range(4)], 0
        )
        send(es, er, CORE_E, CORE_E, core)

        def to_core(jd):
            cs[jd] = numerator(1 - k, jd)
            send(cs.at[jd], cr.at[jd], CORE + jd, CORE + jd, core)

        def to_first(jd):
            value = numerator(k, jd)
            arrived(cr.at[jd], CORE + jd)
            own[jd] = value + cr[jd]
            for d in near:
                for p in range(2):
                    (me, at), (other, _) = axes[p]
                    to, j = (me + d) % 4, (other + jd) % 4
                    send(
                        own.at[jd, rows(p * 64 + to * 16, 16), :], r1.at[p, me, rows(j * 16, 16), :],
                        P1 + p, P1 + p * 4 + j, at(to),
                    )
            for p in range(2):
                (me, _), (other, _) = axes[p]
                j = (other + jd) % 4
                r1[p, me, rows(j * 16, 16), :] = own[jd, rows(p * 64 + me * 16, 16), :]

        to_core(2)
        arrived(er, CORE_E)
        re1[x] = es[...] + er[...]
        exchange_e(E1, re1, x, at_x, 4, near)
        to_core(1)
        to_first(2)
        to_core(3)
        to_first(1)
        to_core(0)
        to_first(3)
        to_first(0)

        for jd in (2, 1, 3, 0):
            if jd == 1:
                arrived(re1.at[0:3], E1)
                re2[y] = (re1[0] + re1[1]) + (re1[2] + re1[3])
                exchange_e(E2, re2, y, at_y, 4, near)
            for p in range(2):
                me, at = axes[p][1]
                j = (me + jd) % 4
                arrived(r1.at[p, 0:3, 0:16, :], P1 + p * 4 + j)
                at_j = rows(j * 16, 16)
                total = (r1[p, 0, at_j, :] + r1[p, 1, at_j, :]) + (r1[p, 2, at_j, :] + r1[p, 3, at_j, :])
                if jd:
                    s2[p, jd] = total
                    send(s2.at[p, jd], r2.at[p, me], P2 + p, P2 + p, at(j))
                else:
                    r2[p, me] = total
        arrived(re2.at[0:3], E2)
        re3[z] = (re2[0] + re2[1]) + (re2[2] + re2[3])
        exchange_e(E3, re3, z, at_z, 8, near_z)

        for p in range(2):
            arrived(r2.at[p, 0:3], P2 + p)
            total = (r2[p, 0] + r2[p, 1]) + (r2[p, 2] + r2[p, 3])
            for i in range(8):
                s3[p, i] = total[(i // 4) * 8 : (i // 4) * 8 + 8, (i % 4) * 128 : (i % 4) * 128 + 128]
            for d in near_z:
                to = (z + d) % 8
                send(s3.at[p, to], r3.at[p, z], P3 + p, P3 + p, at_z(to))
            r3[p, z] = s3[p, z]

        base = [k * 512 + p * 256 + axes[p][0][0] * 64 for p in range(2)]
        small = [base[p] + axes[p][1][0] * 16 for p in range(2)]
        for p in range(2):
            arrived(r3.at[p, 0:7], P3 + p)
            total = ((r3[p, 0] + r3[p, 1]) + (r3[p, 2] + r3[p, 3])) + ((r3[p, 4] + r3[p, 5]) + (r3[p, 6] + r3[p, 7]))
            if p == 0:
                arrived(re3.at[0:7], E3)
                esum[...] = ((re3[0] + re3[1]) + (re3[2] + re3[3])) + ((re3[4] + re3[5]) + (re3[6] + re3[7]))
            tile = (rows(small[p] + tile_row, 8), tile_col)
            dland[tile] = dland[tile] * total / esum[pl.ds(4 + z % 4, 1), :]
            for d in near_z:
                send(dland.at[tile], dland.at[tile], G3 + p, G3 + p, at_z((z + d) % 8))

        esum_v = esum[...]
        set_row(drow[...] * row_of(esum_v[0:4, :]) / row_of(esum_v[4:8, :]))

        def spread(p, jd):
            (me, at), (other, _) = axes[p]
            j = (other + jd) % 4
            piece = dland.at[rows(base[p] + j * 16, 16), :]
            for d in near:
                send(piece, piece, G1 + p, G1 + p * 4 + j, at((me + d) % 4))
            send(piece, piece, GC + p, GC + p * 4 + j, core)

        for p in range(2):
            me, at = axes[p][1]
            piece = dland.at[rows(small[p], 16), :]
            arrived(dland.at[0:56, 0:128], G3 + p)
            for d in near:
                send(piece, piece, G2 + p, G2 + p * 4 + me, at((me + d) % 4))
        for p in range(2):
            spread(p, 0)

        for jd in (1, 3, 2):
            for p in range(2):
                j = (axes[p][1][0] + jd) % 4
                arrived(dland.at[rows(base[p] + j * 16, 16), :], G2 + p * 4 + j)
                spread(p, jd)

        def consume(half, jd):
            @pl.when(t < ITERS - 1)
            def _():
                starts = group(half, jd)
                high, low = split(gather(dland, starts))
                for n, start in enumerate(starts):
                    dbf[rows(start, 16), :] = high[n * 16 : n * 16 + 16, :]
                first_half(high, low, gather(mag, starts))

        def from_core(jd):
            for p in range(2):
                j = (axes[p][1][0] + jd) % 4
                arrived(dland.at[0:64, :], GC + p * 4 + j)
            consume(1 - k, jd)

        @pl.when(t < ITERS - 1)
        def _():
            start_first_half()

        past = None
        for jd in (0, 1, 3, 2):
            for p in range(2):
                (me, _), (other, _) = axes[p]
                j = (other + jd) % 4
                arrived(dland.at[0:48, :], G1 + p * 4 + j)
                for d in (1, 3, 2):
                    i = (me + d) % 4
                    piece = dland.at[rows(k * 512 + p * 256 + i * 64 + j * 16, 16), :]
                    send(piece, piece, GC + p, GC + p * 4 + j, core)
            consume(k, jd)
            if past is not None:
                from_core(past)
            past = jd
        from_core(past)

        @pl.when(t < ITERS - 1)
        def _():
            finish_first_half()

        left(es, CORE_E)
        for jd in range(4):
            left(cs.at[jd], CORE + jd)
        for p in range(2):
            left(dland.at[0:192, :], P1 + p)
            left(dland.at[0:48, :], P2 + p)
            left(s3.at[p, 0:7], P3 + p)
            left(s3.at[p, 0:7], G3 + p)
            left(dland.at[0:48, :], G2 + p)
            left(dland.at[0:192, :], G1 + p)
            left(dland.at[0:256, :], GC + p)
        left(re1.at[0:3], E1)
        left(re2.at[0:3], E2)
        left(re3.at[0:7], E3)

    d_out[0:1024, :] = dland[...]
    d_out[1024:1025, :] = drow[...]


def nmf(wave, dictionary, activations):
    vmem = pl.BlockSpec(memory_space=pltpu.VMEM)
    hbm = pl.BlockSpec(memory_space=pltpu.HBM)
    return pl.pallas_call(
        nmf_kernel,
        out_shape=[
            jax.ShapeDtypeStruct((BINS, K), F32),
            jax.ShapeDtypeStruct((K, 512), F32),
        ],
        in_specs=[hbm, hbm, vmem, hbm, hbm],
        out_specs=[vmem] * 2,
        scratch_shapes=[
            pltpu.VMEM((4104, 128), F32),
            pltpu.VMEM((512, WIN), BF16),
            pltpu.VMEM((8, 128), F32),
            pltpu.VMEM((128, HOP), BF16),
            pltpu.VMEM((2064, WIN), BF16),
            pltpu.VMEM((2064, 512), F32),
            pltpu.VMEM((1025, 512), F32),
            pltpu.VMEM((1024, K), F32),
            pltpu.VMEM((1024, K), BF16),
            pltpu.VMEM((32, K), BF16),
            pltpu.VMEM((1, K), F32),
            pltpu.VMEM((K, 512), BF16),
            pltpu.VMEM((512, K), BF16),
            pltpu.VMEM((K, 512), F32),
            pltpu.VMEM((K, 128), F32),
            pltpu.VMEM((4, 128, K), F32),
            pltpu.VMEM((4, 128, K), F32),
            pltpu.VMEM((8, 128), F32),
            pltpu.VMEM((8, 128), F32),
            pltpu.VMEM((4, 128, K), F32),
            pltpu.VMEM((2, 4, 64, K), F32),
            pltpu.VMEM((2, 4, 16, K), F32),
            pltpu.VMEM((2, 8, 8, 128), F32),
            pltpu.VMEM((2, 4, 16, K), F32),
            pltpu.VMEM((2, 8, 8, 128), F32),
            pltpu.VMEM((4, 8, 128), F32),
            pltpu.VMEM((4, 8, 128), F32),
            pltpu.VMEM((8, 8, 128), F32),
            pltpu.VMEM((8, 128), F32),
            pltpu.SemaphoreType.DMA((SEMS,)),
            pltpu.SemaphoreType.DMA((SEMS,)),
            pltpu.SemaphoreType.DMA((13,)),
            pltpu.SemaphoreType.DMA((2,)),
        ],
        compiler_params=pltpu.CompilerParams(
            collective_id=0, has_side_effects=True, vmem_limit_bytes=58 * 2**20
        ),
        name="nmf",
    )(wave, jnp.asarray(make_table()), jnp.asarray(make_window()), dictionary, activations)


def per_device(wave, dict_init, act_init):
    dictionary, activations = nmf(wave.reshape(-1, 128), dict_init, act_init[0])
    scale = atom_scale(jnp.arange(K, dtype=F32))
    return (dictionary * scale[None, :], (activations * (1.0 / scale)[:, None])[None])


def solution(mesh):
    in_specs = (P("corpus", "tm"), P(), P("corpus", None, "tm"))
    out_specs = (P(), P("corpus", None, "tm"))
    return jax.shard_map(
        per_device, mesh=mesh, in_specs=in_specs, out_specs=out_specs, check_vma=False
    )
```

time: 174 us -> 138 us (0.79)
  other arithmetic: 21.3 us -> 4.39 us
  matrix products: 9.43 us -> 0 us
  local copies, waits for them, and re-layouts: 5 us -> 0.01 us
  Pallas kernels: 136 us -> 133 us
    unnamed x1 -> x0, other arithmetic: 19 us -> none
    dot_general x1 -> x0, matrix products: 9.43 us -> none  [per_device(): lax.dot_general(jnp.asarray(make_table()), frames, (((1,), (1,)), ((), ()...]
    pallas_call x1, Pallas kernels: 136 us -> 133 us  [nmf(): pl.pallas_call(nmf_kernel, out_shape=[jax.ShapeDtypeStruct((BINS, K), F32...]
    mul x0 -> x1, other arithmetic: none -> 3.26 us  [per_device(): dictionary * scale[None, :]]
    unnamed x7 -> x2, local copies, waits for them, and re-layouts: 2.82 us -> 0.01 us
    sqrt x1 -> x0, other arithmetic: 2.22 us -> none  [per_device(): mag = jnp.sqrt(spec[:BINS] ** 2 + spec[BINS:] ** 2 + 0.01)]
  transfers between devices with their start and end apart: 1 -> 0, of which waited for: 0 -> 0; matrix products, arithmetic and copies ran while one was open for 12% -> 0% of each run, Pallas kernels for 0% -> 0%
where the time goes in v2:
time: 138 us
  Pallas kernels  133 us (96%)
  other arithmetic  4.39 us (3%)
    pallas_call x1, Pallas kernels, nmf(): pl.pallas_call(nmf_kernel, out_shape=[jax.ShapeDtypeStruct((BINS, K), F32...  133 us
    mul x1, other arithmetic, per_device(): dictionary * scale[None, :]  3.26 us

profile of v2, /device:TPU:1, one launch (start us, length us, event | category | flops | bytes accessed | tf_op | source)
XLA Modules:
  0.0 137.8 jit_solution(730179061530148687)
XLA Ops:
  0.6 132.8 %nmf.1 = (f32[1025,512]{1,0:T(8,128)}, f32[512,512]{1,0:T(8,128)}) custom-call(f32[4096,128]{1,0:T(8,128)} %bitcast.4, bf16[2064,2048]{1,0:T(8,128)(2,1)} %constant.8.clone.table, f32[16,128]{1,0:T(8,128)} %constant.9.clone.window, f32[1025,512]{1,0:T(8,128)} %d0.1, f32[512,512]{1,0:T(8,128)} %bitcast.5), custom_call_target="tpu_custom_call" | custom-call | tf_op jit(solution)/shard_map/nmf/pallas_call | solution.py:438
  133.4 0.0 copy-start
  133.4 3.3 %broadcast_multiply_fusion = f32[1025,512]{1,0:T(8,128)} fusion(f32[1025,512]{1,0:T(8,128)} %get-tuple-element.4, f32[512]{0:T(512)S(1)} %fusion), kind=kLoop, calls=%fused_computation | loop fusion | flops 524800 | bytes 4200448 | tf_op jit(solution)/shard_map/mul | solution.py:491
  136.7 0.0 copy-done
  136.7 1.1 multiply_bitcast_fusion
  (2 shorter events, 0.0 us)
Async XLA Ops:
  133.4 3.3 %copy-start = (f32[512,512]{1,0:T(8,128)S(1)}, f32[512,512]{1,0:T(8,128)}, u32[]{:S(2)}) copy-start(f32[512,512]{1,0:T(8,128)} %get-tuple-element.5) | copy-start | bytes 3145732

commit v3 on v2

v3 whole, which is shorter than its diff:
```python
import functools

import jax
import jax.numpy as jnp
import numpy as np
from jax import lax
from jax.experimental import pallas as pl
from jax.experimental.pallas import tpu as pltpu
from jax.sharding import PartitionSpec as P

WIN = 2048
HOP = 1024
BINS = 1025
K = 512
ITERS = 3
MESH = pl.DeviceIdType.MESH
F32 = jnp.float32
BF16 = jnp.bfloat16


def make_table():
    index_n = np.arange(WIN, dtype=np.int64)[None, :]
    index_k = np.arange(BINS, dtype=np.int64)[:, None]
    phase = (index_k * index_n % WIN).astype(np.float64) * (2.0 * np.pi / WIN)
    last = np.zeros((16, WIN))
    last[0], last[8] = np.cos(phase[BINS - 1]), np.sin(phase[BINS - 1])
    table = np.concatenate([np.cos(phase[: BINS - 1]), np.sin(phase[: BINS - 1]), last], 0)
    return table.astype(np.float32).astype(jnp.bfloat16)


def make_window():
    index_n = np.arange(WIN, dtype=np.float64)
    return (0.5 - 0.5 * np.cos(2.0 * np.pi * index_n / WIN)).astype(np.float32).reshape(16, 128)


def device(x, y, z, k):
    return (x * 16 + (y // 2) * 8 + z, (y % 2) * 2 + k)


CORE, CORE_E, E1, E2, E3, P3 = 0, 4, 5, 6, 7, 8
P1, P2, G3, G2, G1, GC = 10, 26, 42, 58, 74, 90
SEMS = 106


def atom_scale(index):
    value = index * 0.6180339887
    return 1.0 + (value - jnp.floor(value))


def nmf_kernel(
    wave, table, window, d0, a0, d_result, a_result,
    a_out,    samples, frames, halo, tail, tab, spec, mag,
    dland, debf, drow, abf, atbf, upd, csum,
    cs, cr, es, er, own,
    r1, r2, r3, s2, s3, re1, re2, re3, esum, ssem, rsem, lsem, hsem,
):
    tm, corpus = lax.axis_index("tm"), lax.axis_index("corpus")
    x, z, k = tm // 16, tm % 8, corpus % 2
    y = ((tm // 8) % 2) * 2 + corpus // 2
    core = device(x, y, z, 1 - k)

    def at_x(i):
        return device(i, y, z, k)

    def at_y(i):
        return device(x, i, z, k)

    def at_z(i):
        return device(x, y, i, k)

    axes = (((x, at_x), (y, at_y)), ((y, at_y), (x, at_x)))

    loads = [
        pltpu.make_async_copy(d0.at[0:1024, :], dland, lsem.at[0]),
        pltpu.make_async_copy(a0, a_out, lsem.at[1]),
        pltpu.make_async_copy(d0.at[1024:1025, :], drow, lsem.at[2]),
        pltpu.make_async_copy(table.at[2048:2064, :], tab.at[2048:2064, :], lsem.at[3]),
    ]
    for c in range(4):
        part = slice(c * 512, c * 512 + 512)
        loads.append(pltpu.make_async_copy(table.at[part, :], tab.at[part, :], lsem.at[4 + c]))
    for c in range(4):
        part = slice(c * 1024, c * 1024 + 1024)
        loads.append(pltpu.make_async_copy(wave.at[part, :], samples.at[part, :], lsem.at[8 + c]))
    for i in (8, 9, 10, 11, 4):
        loads[i].start()

    def store(first):
        part = pl.ds(pl.multiple_of(first, 512), 512)
        return dland.at[part, :], d_result.at[part, :]

    stores = [
        pltpu.make_async_copy(a_out, a_result, lsem.at[12]),
        pltpu.make_async_copy(*store(k * 512), lsem.at[13]),
        pltpu.make_async_copy(*store((1 - k) * 512), lsem.at[14]),
        pltpu.make_async_copy(drow, d_result.at[1024:1025, :], lsem.at[15]),
    ]

    barrier = pltpu.get_barrier_semaphore()
    before, after = ((tm + 63) % 64, corpus), ((tm + 1) % 64, corpus)
    for neighbour in (before, after):
        pl.semaphore_signal(barrier, inc=1, device_id=neighbour, device_id_type=MESH)
    pl.semaphore_signal(barrier, inc=1, device_id=core, device_id_type=MESH)
    for d in range(1, 4):
        pl.semaphore_signal(barrier, inc=1, device_id=at_x((x + d) % 4), device_id_type=MESH)
        pl.semaphore_signal(barrier, inc=1, device_id=at_y((y + d) % 4), device_id_type=MESH)
    for d in range(1, 8):
        pl.semaphore_signal(barrier, inc=1, device_id=at_z((z + d) % 8), device_id_type=MESH)

    def copy(src, dst, send, recv, to):
        return pltpu.make_async_remote_copy(
            src_ref=src, dst_ref=dst, send_sem=ssem.at[send], recv_sem=rsem.at[recv],
            device_id=to, device_id_type=MESH,
        )

    def rows(start, count, step=None):
        return pl.ds(pl.multiple_of(start, step or count), count)

    def dot(a, b):
        return jnp.dot(a, b, preferred_element_type=F32)

    def dot_t(a, b):
        return lax.dot_general(a, b, (((0,), (0,)), ((), ())), preferred_element_type=F32)

    def dot_nt(a, b):
        return lax.dot_general(a, b, (((1,), (1,)), ((), ())), preferred_element_type=F32)

    def split(value):
        high = value.astype(BF16)
        return high, (value - high.astype(F32)).astype(BF16)

    row_id = lax.broadcasted_iota(jnp.int32, (16, K), 0)

    def row_of(tile):
        return jnp.concatenate([tile[i : i + 1, :] for i in range(4)], 1)

    def ratio_e():
        approx = dot(debf[0:16, :], abf[...])
        return mag[1024:1025, :] / approx[0:1, :]

    def set_row(row):
        drow[...] = row
        high, low = split(jnp.where(row_id == 0, row, 0.0))
        debf[0:16, :] = high
        debf[16:32, :] = low

    def products(high, low, ratio):
        rh, rl = split(ratio)
        left = jnp.concatenate([high, high, low], 0)
        update = dot_t(left, jnp.concatenate([rh, rl, rh], 0))
        count = high.shape[0]
        return update, dot_t(left[count:], jnp.ones((2 * count, 128), BF16))

    def first_half(high, low, target):
        ratio = target / dot(high, abf[...])
        update, total = products(high, low, ratio)
        upd[...] += update
        csum[...] += total

    def start_first_half():
        ratio = jnp.where(row_id == 0, ratio_e(), 0.0)
        update, total = products(debf[0:16, :], debf[16:32, :], ratio)
        upd[...] = update
        csum[...] = total

    def set_act():
        value = a_out[...]
        abf[...] = value.astype(BF16)
        atbf[...] = value.T.astype(BF16)

    def finish_first_half():
        scale = 1.0 / csum[...]
        for i in range(4):
            cols = slice(i * 128, i * 128 + 128)
            a_out[:, cols] = a_out[:, cols] * upd[:, cols] * scale
        set_act()

    def build(c, second):
        for i in range(8):
            start = c * 1024 + second * 8 + i
            value = samples[pl.ds(start, 128, stride=8), :] * window[second * 8 + i : second * 8 + i + 1, :]
            cols = slice(second * 1024 + i * 128, second * 1024 + i * 128 + 128)
            frames[c * 128 : c * 128 + 128, cols] = value.astype(BF16)

    samples[4096:4104, :] = jnp.zeros((8, 128), F32)
    for c in range(4):
        loads[8 + c].wait()
        build(c, 0)
        if c:
            build(c - 1, 1)
    for i in (5, 6, 7, 3, 1, 0, 2):
        loads[i].start()
    build(3, 1)

    for c in range(4):
        if c == 1:
            pl.semaphore_wait(barrier, 16)
            greet = pltpu.make_async_remote_copy(
                src_ref=samples.at[0:8, :], dst_ref=halo, send_sem=hsem.at[0], recv_sem=hsem.at[1],
                device_id=before, device_id_type=MESH,
            )
            greet.start()
        part = slice(c * 512, c * 512 + 512)
        loads[4 + c].wait()
        spec[part, :] = dot_nt(tab[part, :], frames[...])
    loads[3].wait()
    spec[2048:2064, :] = dot_nt(tab[2048:2064, :], frames[...])

    for i in range(3):
        loads[i].wait()
    atom_row = lax.broadcasted_iota(jnp.int32, (8, K), 1).astype(F32)[0:1]
    atom_col = lax.broadcasted_iota(jnp.int32, (K, 128), 0).astype(F32)
    inverse = 1.0 / atom_scale(atom_row)
    scale = atom_scale(atom_col)
    for i in range(4):
        cols = slice(i * 128, i * 128 + 128)
        value = a_out[:, cols] * scale
        a_out[:, cols] = value
        abf[:, cols] = value.astype(BF16)

    set_row(drow[...] * inverse)

    greet.wait()
    keep = jnp.where(tm == 63, 0.0, 1.0)
    tail[...] = jnp.zeros((128, 1024), BF16)
    last = halo[...] * window[8:16, :] * keep
    last = jnp.concatenate([last[c : c + 1, :] for c in range(8)], 1)
    row_16 = lax.broadcasted_iota(jnp.int32, (16, 1024), 0)
    tail[112:128, :] = jnp.where(row_16 == 15, last, 0.0).astype(BF16)
    spec[:, 384:512] += dot_nt(tab[:, 1024:2048], tail[...])

    real, imag = spec[2048:2049, :], spec[2056:2057, :]
    mag[1024:1025, :] = jnp.sqrt(real * real + imag * imag + 0.01)
    start_first_half()

    @pl.loop(0, 4)
    def _(c):
        real, imag = spec[rows(c * 256, 256), :], spec[rows(1024 + c * 256, 256), :]
        target = jnp.sqrt(real * real + imag * imag + 0.01)
        mag[rows(c * 256, 256), :] = target
        value = dland[rows(c * 256, 256), :] * inverse
        dland[rows(c * 256, 256), :] = value
        high, low = split(value)
        first_half(high, low, target)

    finish_first_half()

    near = (2, 1, 3)
    near_z = (4, 3, 5, 2, 6, 1, 7)
    pairs = ((4, 3), (5, 2), (6, 1), (7, 0))

    @pl.loop(0, ITERS)
    def _(t):
        def send(*args):
            copy(*args).start()

        def arrived(dst, recv):
            copy(dst, dst, 0, recv, core).wait_recv()

        def left(src, sent):
            copy(src, src, sent, 0, core).wait_send()

        def block(half, p, i, zz):
            return half * 512 + p * 256 + i * 64 + zz * 8

        def group(half, g):
            return [
                block(half, p, i, (z + zd) % 8) for p in range(2) for i in range(4) for zd in pairs[g]
            ]

        def gather(ref, starts):
            return jnp.concatenate([ref[rows(start, 8), :] for start in starts], 0)

        def numerator(half, g):
            starts = group(half, g)
            ratio = gather(mag, starts) / dot(gather(dland, starts).astype(BF16), abf[...])
            return dot(ratio.astype(BF16), atbf[...])

        def exchange_e(sem, dst, me, at, count, order):
            for d in order:
                send(dst.at[me], dst.at[me], sem, sem, at((me + d) % count))


        def to_core(g):
            cs[g] = numerator(1 - k, g)
            send(cs.at[g], cr.at[g], CORE + g, CORE + g, core)

        def to_first(g):
            value = numerator(k, g)
            arrived(cr.at[g], CORE + g)
            own[g] = value + cr[g]
            for q in range(2):
                zz = (z + pairs[g][q]) % 8
                for d in near:
                    for p in range(2):
                        me, at = axes[p][0]
                        to = (me + d) % 4
                        send(
                            own.at[g, rows(p * 64 + to * 16 + q * 8, 8), :], r1.at[p, me, zz],
                            P1 + p, P1 + p * 8 + zz, at(to),
                        )
            for q in range(2):
                zz = (z + pairs[g][q]) % 8
                for p in range(2):
                    me = axes[p][0][0]
                    r1[p, me, zz] = own[g, rows(p * 64 + me * 16 + q * 8, 8), :]

        def to_second(zd):
            zz = (z + zd) % 8
            for p in range(2):
                me, at = axes[p][1]
                arrived(dland.at[0:24, :], P1 + p * 8 + zz)
                total = (r1[p, 0, zz] + r1[p, 1, zz]) + (r1[p, 2, zz] + r1[p, 3, zz])
                for j in range(4):
                    s2[p, zz, j] = total[:, j * 128 : j * 128 + 128]
                for d in near:
                    to = (me + d) % 4
                    send(s2.at[p, zz, to], r2.at[p, me, zz], P2 + p, P2 + p * 8 + zz, at(to))
                r2[p, me, zz] = s2[p, zz, me]

        def to_third(zd):
            zz = (z + zd) % 8
            for p in range(2):
                arrived(s3.at[p, 0:3], P2 + p * 8 + zz)
                total = (r2[p, 0, zz] + r2[p, 1, zz]) + (r2[p, 2, zz] + r2[p, 3, zz])
                if zd:
                    s3[p, zz] = total
                    send(s3.at[p, zz], r3.at[p, z], P3 + p, P3 + p, at_z(zz))
                else:
                    r3[p, z] = total

        to_core(0)
        ratio = jnp.where(row_id == 0, ratio_e(), jnp.where(row_id == 8, 1.0, 0.0)).astype(BF16)
        line = dot(ratio, atbf[...])
        es[...] = jnp.concatenate(
            [line[r : r + 1, i * 128 : i * 128 + 128] for r in (0, 8) for i in range(4)], 0
        )
        send(es, er, CORE_E, CORE_E, core)
        to_core(1)
        arrived(er, CORE_E)
        re1[x] = es[...] + er[...]
        exchange_e(E1, re1, x, at_x, 4, near)
        to_first(0)
        to_core(2)
        to_first(1)
        to_core(3)
        to_first(2)
        to_first(3)

        arrived(re1.at[0:3], E1)
        re2[y] = (re1[0] + re1[1]) + (re1[2] + re1[3])
        exchange_e(E2, re2, y, at_y, 4, near)
        for zd in (4, 3, 5, 2, 6):
            to_second(zd)
        arrived(re2.at[0:3], E2)
        re3[z] = (re2[0] + re2[1]) + (re2[2] + re2[3])
        exchange_e(E3, re3, z, at_z, 8, near_z)
        to_third(4)
        to_second(1)
        to_third(3)
        to_second(7)
        to_third(5)
        to_second(0)
        for zd in (2, 6, 1, 7, 0):
            to_third(zd)

        def tile_of(p, zz):
            (me, _), (other, _) = axes[p]
            return dland.at[rows(block(k, p, me, zz), 8), pl.ds(pl.multiple_of(other * 128, 128), 128)]

        for p in range(2):
            arrived(r3.at[p, 0:7], P3 + p)
            total = ((r3[p, 0] + r3[p, 1]) + (r3[p, 2] + r3[p, 3])) + ((r3[p, 4] + r3[p, 5]) + (r3[p, 6] + r3[p, 7]))
            if p == 0:
                arrived(re3.at[0:7], E3)
                esum[...] = ((re3[0] + re3[1]) + (re3[2] + re3[3])) + ((re3[4] + re3[5]) + (re3[6] + re3[7]))
            tile = tile_of(p, z)
            tile[...] = tile[...] * total / esum[pl.ds(4 + axes[p][1][0], 1), :]
            for d in near_z:
                send(tile, tile, G3 + p, G3 + p * 8 + z, at_z((z + d) % 8))

        def along_second(zd):
            zz = (z + zd) % 8
            for p in range(2):
                me, at = axes[p][1]
                tile = tile_of(p, zz)
                if zd:
                    arrived(tile, G3 + p * 8 + zz)
                for d in near:
                    send(tile, tile, G2 + p, G2 + p * 8 + zz, at((me + d) % 4))

        def along_first(zd):
            zz = (z + zd) % 8
            for p in range(2):
                me, at = axes[p][0]
                arrived(dland.at[0:24, 0:128], G2 + p * 8 + zz)
                piece = dland.at[rows(block(k, p, me, zz), 8), :]
                for d in near:
                    send(piece, piece, G1 + p, G1 + p * 8 + zz, at((me + d) % 4))
                send(piece, piece, GC + p, GC + p * 8 + zz, core)

        along_second(0)
        esum_v = esum[...]
        set_row(drow[...] * row_of(esum_v[0:4, :]) / row_of(esum_v[4:8, :]))

        for zd in (1, 7, 2, 6):
            along_second(zd)
        along_first(0)
        for zd in (3, 5, 4):
            along_second(zd)
        for zd in (1, 7, 2, 6, 3, 5, 4):
            along_first(zd)

        def consume(half, g):
            @pl.when(t < ITERS - 1)
            def _():
                starts = group(half, g)
                high, low = split(gather(dland, starts))
                first_half(high, low, gather(mag, starts))

        def across(*distances):
            for zd in distances:
                zz = (z + zd) % 8
                for p in range(2):
                    me = axes[p][0][0]
                    arrived(dland.at[0:24, :], G1 + p * 8 + zz)
                    for d in (1, 3, 2):
                        piece = dland.at[rows(block(k, p, (me + d) % 4, zz), 8), :]
                        send(piece, piece, GC + p, GC + p * 8 + zz, core)

        def from_core(g):
            for zd in pairs[g]:
                zz = (z + zd) % 8
                for p in range(2):
                    arrived(dland.at[0:32, :], GC + p * 8 + zz)
            consume(1 - k, g)

        @pl.when(t < ITERS - 1)
        def _():
            start_first_half()

        across(0, 1, 7)
        consume(k, 3)
        across(2, 6)
        consume(k, 2)
        from_core(3)
        across(3, 5)
        consume(k, 1)
        from_core(2)
        across(4)

        @pl.when(t == ITERS - 1)
        def _():
            stores[1].start()

        consume(k, 0)
        from_core(1)
        from_core(0)

        @pl.when(t < ITERS - 1)
        def _():
            finish_first_half()

        @pl.when(t == ITERS - 2)
        def _():
            stores[0].start()

        left(es, CORE_E)
        for g in range(4):
            left(cs.at[g], CORE + g)
        for p in range(2):
            left(dland.at[0:192, :], P1 + p)
            left(dland.at[0:192, 0:128], P2 + p)
            left(s3.at[p, 0:7], P3 + p)
            left(s3.at[p, 0:7], G3 + p)
            left(dland.at[0:192, 0:128], G2 + p)
            left(dland.at[0:192, :], G1 + p)
            left(dland.at[0:256, :], GC + p)
        left(re1.at[0:3], E1)
        left(re2.at[0:3], E2)
        left(re3.at[0:7], E3)

    stores[2].start()
    stores[3].start()
    for copied in stores:
        copied.wait()


def nmf(wave, dictionary, activations):
    vmem = pl.BlockSpec(memory_space=pltpu.VMEM)
    hbm = pl.BlockSpec(memory_space=pltpu.HBM)
    return pl.pallas_call(
        nmf_kernel,
        out_shape=[
            jax.ShapeDtypeStruct((BINS, K), F32),
            jax.ShapeDtypeStruct((K, 512), F32),
        ],
        in_specs=[hbm, hbm, vmem, hbm, hbm],
        out_specs=[hbm] * 2,
        scratch_shapes=[
            pltpu.VMEM((K, 512), F32),
            pltpu.VMEM((4104, 128), F32),
            pltpu.VMEM((512, WIN), BF16),
            pltpu.VMEM((8, 128), F32),
            pltpu.VMEM((128, HOP), BF16),
            pltpu.VMEM((2064, WIN), BF16),
            pltpu.VMEM((2064, 512), F32),
            pltpu.VMEM((1025, 512), F32),
            pltpu.VMEM((1024, K), F32),
            pltpu.VMEM((32, K), BF16),
            pltpu.VMEM((1, K), F32),
            pltpu.VMEM((K, 512), BF16),
            pltpu.VMEM((512, K), BF16),
            pltpu.VMEM((K, 512), F32),
            pltpu.VMEM((K, 128), F32),
            pltpu.VMEM((4, 128, K), F32),
            pltpu.VMEM((4, 128, K), F32),
            pltpu.VMEM((8, 128), F32),
            pltpu.VMEM((8, 128), F32),
            pltpu.VMEM((4, 128, K), F32),
            pltpu.VMEM((2, 4, 8, 8, K), F32),
            pltpu.VMEM((2, 4, 8, 8, 128), F32),
            pltpu.VMEM((2, 8, 8, 128), F32),
            pltpu.VMEM((2, 8, 4, 8, 128), F32),
            pltpu.VMEM((2, 8, 8, 128), F32),
            pltpu.VMEM((4, 8, 128), F32),
            pltpu.VMEM((4, 8, 128), F32),
            pltpu.VMEM((8, 8, 128), F32),
            pltpu.VMEM((8, 128), F32),
            pltpu.SemaphoreType.DMA((SEMS,)),
            pltpu.SemaphoreType.DMA((SEMS,)),
            pltpu.SemaphoreType.DMA((16,)),
            pltpu.SemaphoreType.DMA((2,)),
        ],
        compiler_params=pltpu.CompilerParams(
            collective_id=0, has_side_effects=True, vmem_limit_bytes=58 * 2**20
        ),
        name="nmf",
    )(wave, jnp.asarray(make_table()), jnp.asarray(make_window()), dictionary, activations)


def unscale_kernel(d, a, d_result, a_result, dv, av, sem_in, sem_out):
    parts = [(d, dv, d_result, slice(c * 256, c * 256 + 256)) for c in range(4)]
    parts += [(a, av, a_result, slice(c * 256, c * 256 + 256)) for c in range(2)]
    parts += [(d, dv, d_result, slice(1024, 1025))]
    loads = [
        pltpu.make_async_copy(source.at[part, :], held.at[part, :], sem_in.at[n])
        for n, (source, held, _, part) in enumerate(parts)
    ]
    stores = [
        pltpu.make_async_copy(held.at[part, :], result.at[part, :], sem_out.at[n])
        for n, (_, held, result, part) in enumerate(parts)
    ]
    for load in loads:
        load.start()
    atom_row = atom_scale(lax.broadcasted_iota(jnp.int32, (8, K), 1).astype(F32)[0:1])
    for n, (_, held, _, part) in enumerate(parts):
        loads[n].wait()
        if held is dv:
            dv[part, :] = dv[part, :] * atom_row
        else:
            atom_col = (lax.broadcasted_iota(jnp.int32, (256, 128), 0) + part.start).astype(F32)
            inverse = 1.0 / atom_scale(atom_col)
            for i in range(4):
                cols = slice(i * 128, i * 128 + 128)
                av[part, cols] = av[part, cols] * inverse
        stores[n].start()
    for store in stores:
        store.wait()


def unscale(dictionary, activations):
    hbm = pl.BlockSpec(memory_space=pltpu.HBM)
    return pl.pallas_call(
        unscale_kernel,
        out_shape=[
            jax.ShapeDtypeStruct((BINS, K), F32),
            jax.ShapeDtypeStruct((K, 512), F32),
        ],
        in_specs=[hbm] * 2,
        out_specs=[hbm] * 2,
        scratch_shapes=[
            pltpu.VMEM((BINS, K), F32),
            pltpu.VMEM((K, 512), F32),
            pltpu.SemaphoreType.DMA((7,)),
            pltpu.SemaphoreType.DMA((7,)),
        ],
        compiler_params=pltpu.CompilerParams(vmem_limit_bytes=58 * 2**20),
        name="unscale",
    )(dictionary, activations)


def per_device(wave, dict_init, act_init):
    dictionary, activations = unscale(*nmf(wave.reshape(-1, 128), dict_init, act_init[0]))
    return (dictionary, activations[None])


def solution(mesh):
    in_specs = (P("corpus", "tm"), P(), P("corpus", None, "tm"))
    out_specs = (P(), P("corpus", None, "tm"))
    return jax.shard_map(
        per_device, mesh=mesh, in_specs=in_specs, out_specs=out_specs, check_vma=False
    )
```

time: 138 us -> 132 us (0.957)
  other arithmetic: 4.39 us -> 0 us
  Pallas kernels: 133 us -> 131 us
    pallas_call x1, Pallas kernels: 133 us -> 128 us  [nmf(): pl.pallas_call(nmf_kernel, out_shape=[jax.ShapeDtypeStruct((BINS, K), F32...]
    mul x1 -> x0, other arithmetic: 3.26 us -> none  [per_device(): dictionary * scale[None, :]]
    pallas_call x0 -> x1, Pallas kernels: none -> 2.86 us  [unscale(): pl.pallas_call(unscale_kernel, out_shape=[jax.ShapeDtypeStruct((BINS, K),...]
where the time goes in v3:
time: 132 us
  Pallas kernels  131 us (99%)
    pallas_call x1, Pallas kernels, nmf(): pl.pallas_call(nmf_kernel, out_shape=[jax.ShapeDtypeStruct((BINS, K), F32...  128 us
    pallas_call x1, Pallas kernels, unscale(): pl.pallas_call(unscale_kernel, out_shape=[jax.ShapeDtypeStruct((BINS, K),...  2.86 us

profile of v3, /device:TPU:1, one launch (start us, length us, event | category | flops | bytes accessed | tf_op | source)
XLA Modules:
  0.0 131.7 jit_solution(14553419786604745245)
XLA Ops:
  0.6 128.1 %nmf.1 = (f32[1025,512]{1,0:T(8,128)}, f32[512,512]{1,0:T(8,128)}) custom-call(f32[4096,128]{1,0:T(8,128)} %bitcast.3, bf16[2064,2048]{1,0:T(8,128)(2,1)} %constant.4.clone.table, f32[16,128]{1,0:T(8,128)} %constant.5.clone.window, f32[1025,512]{1,0:T(8,128)} %d0.1, f32[512,512]{1,0:T(8,128)} %bitcast.4), custom_call_target="tpu_custom_call" | custom-call | tf_op jit(solution)/shard_map/nmf/pallas_call | solution.py:492
  128.7 2.9 %unscale.1 = (f32[1025,512]{1,0:T(8,128)}, f32[512,512]{1,0:T(8,128)}) custom-call(f32[1025,512]{1,0:T(8,128)} %get-tuple-element.6.d, f32[512,512]{1,0:T(8,128)} %get-tuple-element.7.a), custom_call_target="tpu_custom_call" | custom-call | tf_op jit(solution)/shard_map/unscale/pallas_call | solution.py:574

commit v4 on v3

--- a/solution.py
+++ b/solution.py
@@ -146,22 +146,17 @@
 
     def products(high, low, ratio):
         rh, rl = split(ratio)
-        left = jnp.concatenate([high, high, low], 0)
-        update = dot_t(left, jnp.concatenate([rh, rl, rh], 0))
-        count = high.shape[0]
-        return update, dot_t(left[count:], jnp.ones((2 * count, 128), BF16))
+        return dot_t(jnp.concatenate([high, high, low], 0), jnp.concatenate([rh, rl, rh], 0))
 
     def first_half(high, low, target):
         ratio = target / dot(high, abf[...])
-        update, total = products(high, low, ratio)
-        upd[...] += update
-        csum[...] += total
+        upd[...] += products(high, low, ratio)
+        csum[...] += jnp.sum(high.astype(F32) + low.astype(F32), 0, keepdims=True)
 
     def start_first_half():
         ratio = jnp.where(row_id == 0, ratio_e(), 0.0)
-        update, total = products(debf[0:16, :], debf[16:32, :], ratio)
-        upd[...] = update
-        csum[...] = total
+        upd[...] = products(debf[0:16, :], debf[16:32, :], ratio)
+        csum[...] = drow[...]
 
     def set_act():
         value = a_out[...]
@@ -169,7 +164,7 @@
         atbf[...] = value.T.astype(BF16)
 
     def finish_first_half():
-        scale = 1.0 / csum[...]
+        scale = jnp.broadcast_to(1.0 / csum[...], (128, K)).T
         for i in range(4):
             cols = slice(i * 128, i * 128 + 128)
             a_out[:, cols] = a_out[:, cols] * upd[:, cols] * scale
@@ -192,7 +187,7 @@
         loads[i].start()
     build(3, 1)
 
-    for c in range(4):
+    for c, (first, last, needed) in enumerate(((0, 512, (4,)), (512, 2064, (5, 6, 7, 3)))):
         if c == 1:
             pl.semaphore_wait(barrier, 16)
             greet = pltpu.make_async_remote_copy(
@@ -200,11 +195,9 @@
                 device_id=before, device_id_type=MESH,
             )
             greet.start()
-        part = slice(c * 512, c * 512 + 512)
-        loads[4 + c].wait()
-        spec[part, :] = dot_nt(tab[part, :], frames[...])
-    loads[3].wait()
-    spec[2048:2064, :] = dot_nt(tab[2048:2064, :], frames[...])
+        for i in needed:
+            loads[i].wait()
+        spec[first:last, :] = dot_nt(tab[first:last, :], frames[...])
 
     for i in range(3):
         loads[i].wait()
@@ -233,8 +226,7 @@
     mag[1024:1025, :] = jnp.sqrt(real * real + imag * imag + 0.01)
     start_first_half()
 
-    @pl.loop(0, 4)
-    def _(c):
+    for c in range(4):
         real, imag = spec[rows(c * 256, 256), :], spec[rows(1024 + c * 256, 256), :]
         target = jnp.sqrt(real * real + imag * imag + 0.01)
         mag[rows(c * 256, 256), :] = target
@@ -512,7 +504,7 @@
             pltpu.VMEM((K, 512), BF16),
             pltpu.VMEM((512, K), BF16),
             pltpu.VMEM((K, 512), F32),
-            pltpu.VMEM((K, 128), F32),
+            pltpu.VMEM((1, K), F32),
             pltpu.VMEM((4, 128, K), F32),
             pltpu.VMEM((4, 128, K), F32),
             pltpu.VMEM((8, 128), F32),

time: 132 us -> 131 us (level)
  no operation moved by 1% of the time
where the time goes in v4:
time: 131 us
  Pallas kernels  130 us (99%)
    pallas_call x1, Pallas kernels, nmf(): pl.pallas_call(nmf_kernel, out_shape=[jax.ShapeDtypeStruct((BINS, K), F32...  127 us
    pallas_call x1, Pallas kernels, unscale(): pl.pallas_call(unscale_kernel, out_shape=[jax.ShapeDtypeStruct((BINS, K),...  2.86 us

profile of v4, /device:TPU:1, one launch (start us, length us, event | category | flops | bytes accessed | tf_op | source)
XLA Modules:
  0.0 131.0 jit_solution(8349927990507605281)
XLA Ops:
  0.6 127.3 %nmf.1 = (f32[1025,512]{1,0:T(8,128)}, f32[512,512]{1,0:T(8,128)}) custom-call(f32[4096,128]{1,0:T(8,128)} %bitcast.3, bf16[2064,2048]{1,0:T(8,128)(2,1)} %constant.4.clone.table, f32[16,128]{1,0:T(8,128)} %constant.5.clone.window, f32[1025,512]{1,0:T(8,128)} %d0.1, f32[512,512]{1,0:T(8,128)} %bitcast.4), custom_call_target="tpu_custom_call" | custom-call | tf_op jit(solution)/shard_map/nmf/pallas_call | solution.py:484
  128.0 2.9 %unscale.1 = (f32[1025,512]{1,0:T(8,128)}, f32[512,512]{1,0:T(8,128)}) custom-call(f32[1025,512]{1,0:T(8,128)} %get-tuple-element.6.d, f32[512,512]{1,0:T(8,128)} %get-tuple-element.7.a), custom_call_target="tpu_custom_call" | custom-call | tf_op jit(solution)/shard_map/unscale/pallas_call | solution.py:566
